TPU v7x, 256 devices: a whole 4x4x8 slice. The times are simulated.
256 devices in a mesh: band: 4 (over y), img: 64 (over z, x, core).
Axes of the slice: x: 4, y: 4, z: 8, core: 2. Of those that a mesh axis runs over, the one named last changes fastest.
Arguments:
- images: bfloat16 [4, 1024, 3328], P('band', 'img'), may hold values from -12 to 12
- references: bfloat16 [4, 256, 3328], P('band', 'img'), may hold values from -0.08 to 0.08
- noise_weight: float32 [4, 1664], P('band'), may hold values from 0.5 to 4
- masks: int32 [4, 128, 64, 49], P('band', 'img'), may hold values from 0 to 1, as said below
Outputs:
- weighted_sums: float32 [4, 256, 3328], P('band', 'img')
- weight_totals: float32 [256], P('img')
Inputs may be any that keep to these rules, and one draw needn't show every extreme that they name: `masks`: each entry is 0 or 1; translation number 49 // 2 is kept in every band, image block and orientation block.
All inputs are finite; a program needn't handle non-finite values.
Results may differ from a plain program's by a relative error of at most 0.0065.
Values may be sent and summed in bfloat16 or wider, within the bound.
A program may use at most 64 MiB of HBM per device.

v0:
```python
import math

import jax
import jax.numpy as jnp
from jax import lax
from jax.sharding import PartitionSpec as P

BOX = 256
SIDE = 7
IMG_BLOCK = 8


PENALTY = 10000.0


def shift_angles(band, coef):
    index = jnp.arange(coef, dtype=jnp.int32)
    freq_x = (index * 37 + band * 11) % 257 - 128
    freq_y = (index * 61 + band * 29) % 129
    shift_ids = jnp.arange(SIDE * SIDE, dtype=jnp.int32)
    move_x = shift_ids // SIDE - SIDE // 2
    move_y = shift_ids % SIDE - SIDE // 2
    phase = (move_x[:, None] * freq_x[None, :] + move_y[:, None] * freq_y[None, :]).astype(
        jnp.float32
    )
    angle = phase * (2.0 * math.pi / BOX)
    return (jnp.cos(angle), jnp.sin(angle))


def align(pictures, cosine, sine):
    coef = cosine.shape[1]
    real = pictures[:, :coef].astype(jnp.float32)[:, None, :]
    imag = pictures[:, coef:].astype(jnp.float32)[:, None, :]
    out_real = real * cosine[None] - imag * sine[None]
    out_imag = real * sine[None] + imag * cosine[None]
    joined = jnp.concatenate([out_real, out_imag], axis=2).astype(jnp.bfloat16)
    return joined.reshape(pictures.shape[0] * cosine.shape[0], 2 * coef)


def prepare(projections, weight):
    doubled = jnp.concatenate([weight, weight])
    values = projections.astype(jnp.float32)
    weighted = (values * doubled[None, :]).astype(jnp.bfloat16)
    norms = jnp.sum(values * values * doubled[None, :], axis=1)
    return (weighted, norms)


def penalty(mask_block, img_block, orient_dev):
    blocks, owners, shift_count = mask_block.shape
    dropped = PENALTY * (1 - mask_block).astype(jnp.float32)
    dropped = jnp.transpose(dropped, (0, 2, 1))
    dropped = jnp.broadcast_to(
        dropped[:, None, :, :, None], (blocks, img_block, shift_count, owners, orient_dev)
    )
    return dropped.reshape(blocks * img_block * shift_count, owners * orient_dev)


def band_term(aligned, weighted, norms, dropped):
    cross = lax.dot_general(
        aligned, weighted, (((1,), (1,)), ((), ())), preferred_element_type=jnp.float32
    )
    return cross - 0.5 * norms[None, :] - dropped


def posterior(total, count):
    grid = total.reshape(count, -1)
    peak = jnp.max(grid, axis=1, keepdims=True)
    raised = jnp.exp(grid - peak)
    return (raised / jnp.sum(raised, axis=1, keepdims=True)).reshape(total.shape)


def combine_bands(partial_score):
    total = lax.psum(partial_score, "band")
    return total


def per_device(images, references, noise_weight, masks):
    band_index = lax.axis_index("band")
    coef = noise_weight.shape[1]
    cosine, sine = shift_angles(band_index, coef)
    weight = noise_weight[0]
    owned_refs = references[0]
    owned = owned_refs.shape[0]
    local_images = images[0]
    count = local_images.shape[0]
    aligned = align(local_images, cosine, sine)
    dropped = penalty(masks[0], IMG_BLOCK, owned)
    weighted, norms = prepare(lax.all_gather(references, "img", axis=1, tiled=True)[0], weight)
    partial_score = band_term(aligned, weighted, norms, dropped)
    score = combine_bands(partial_score)
    prob = posterior(score, count)
    post = prob.astype(jnp.bfloat16)
    totals = jnp.sum(prob, axis=0)
    sums = lax.dot_general(
        post, aligned, (((0,), (0,)), ((), ())), preferred_element_type=jnp.float32
    )
    mine_sums, mine_totals = (
        lax.psum_scatter(sums, "img", scatter_dimension=0, tiled=True),
        lax.psum_scatter(totals, "img", scatter_dimension=0, tiled=True),
    )
    return (mine_sums[None], mine_totals)


def solution(mesh):
    in_specs = (
        P("band", "img", None),
        P("band", "img", None),
        P("band", None),
        P("band", "img", None, None),
    )
    out_specs = (P("band", "img", None), P("img"))
    return jax.shard_map(
        per_device, mesh=mesh, in_specs=in_specs, out_specs=out_specs, check_vma=False
    )
```

profile of v0, /device:TPU:1, one launch (start us, length us, event | category | flops | bytes accessed | tf_op | source)
XLA Modules:
  0.0 363.7 jit_solution(10916949939306308659)
XLA Ops:
  7.2 1.4 copy.12
  8.7 0.9 slice_convert_fusion.1
  9.6 1.4 fusion.17
  11.0 3.4 add_convert_fusion
  14.4 3.4 sub.60
  17.8 1.9 add.100
  19.8 1.5 broadcast_in_dim.4
  21.3 2.5 reshape.205
  23.8 1.2 copy.14
  25.1 1.7 constant_dynamic-update-slice_fusion.1
  26.8 0.9 copy-done.2
  27.8 1.7 constant_dynamic-update-slice_fusion
  29.5 64.4 %all-gather.2.cloned.1.call-done = bf16[1,256,3328]{2,0,1:T(2,128)(2,1)} async-done(((bf16[1,4,3328]{2,0,1:T(2,128)(2,1)}), bf16[1,256,3328]{2,0,1:T(2,128)(2,1)}) %all-gather.2.cloned.1.call-update) | async-done | bytes 1703952 | tf_op jit(solution)/shard_map/all_gather | solution.py:88
  93.9 5.5 %convert_element_type.42 = f32[1,256,3328]{2,0,1:T(1,128)S(1)} convert(bf16[1,256,3328]{2,0,1:T(2,128)(2,1)} %all-gather.2.cloned.1.call-done) | non-fusion elementwise | flops 851968 | bytes 5111808 | tf_op jit(solution)/shard_map/convert_element_type | solution.py:42
  99.8 0.7 copy-done.3
  100.5 4.9 %fusion.9 = f32[784,256]{1,0:T(8,128)} fusion(f32[784,256]{1,0:T(8,128)S(1)} %copy-done.3, bf16[784,3328]{1,0:T(8,128)(2,1)} %constant_dynamic-update-slice_fusion, f32[1,256,3328]{2,0,1:T(1,128)S(1)} %convert_element_type.42, f32[3328]{0:T(1024)S(1)} %pad_maximum_fusion, f32[256]{0:T(256)S(1)} %broadcast_multiply_fusion), kind=kOutput, calls=%fused_computation.10 | convolution fusion | flops 1337991168 | bytes 10246144 | tf_op jit(solution)/shard_map/dot_general | solution.py:59
  105.7 44.4 %all-reduce.5.cloned.1.call-done = f32[784,256]{1,0:T(8,128)} async-done(((f32[784,256]{1,0:T(8,128)}), f32[784,256]{1,0:T(8,128)}) %all-reduce.5.cloned.1.call-update) | async-done | bytes 802832 | tf_op jit(solution)/shard_map/psum | solution.py:73
  150.1 1.3 reduce_max.10
  151.8 1.5 fusion.13
  153.7 6.6 %fusion.14 = f32[256,3328]{1,0:T(8,128)} fusion(bf16[784,3328]{1,0:T(8,128)(2,1)} %constant_dynamic-update-slice_fusion, f32[784,256]{1,0:T(8,128)} %all-reduce.5.cloned.1.call-done, f32[784]{0:T(1024)S(1)} %div.25, f32[784]{0:T(1024)S(1)} %sub.67), kind=kOutput, calls=%fused_computation.14 | convolution fusion | flops 1336487936 | bytes 9435264 | tf_op jit(solution)/shard_map/dot_general | solution.py:94
  160.3 0.6 copy-done.6
  162.5 127.2 %all-reduce.1 = f32[256]{0:T(256)S(1)} all-reduce(f32[256]{0:T(256)S(1)} %fusion.27), channel_id=3, replica_groups=mesh['band'=4,'img'=64] {'img'}, use_global_device_ids=true, to_apply=%region_8.9.clone | all-reduce | flops 256 | bytes 2048
  290.3 65.3 %all-reduce.7.cloned.1.call-done = f32[256,3328]{1,0:T(8,128)} async-done(((f32[256,3328]{1,0:T(8,128)}), f32[256,3328]{1,0:T(8,128)}) %all-reduce.7.cloned.1.call-update) | async-done | bytes 3407888
  355.6 1.5 dynamic-slice_bitcast_fusion
  (36 shorter events, 3.2 us)
Async XLA Ops:
  7.2 86.7 %all-gather.2.cloned.1.call-start = ((), (), s32[]{:S(2)}) async-start(), calls=%async_computation | async-start | bytes 3461120 | tf_op jit(solution)/shard_map/all_gather | solution.py:88
  8.6 141.5 %all-reduce.5.cloned.1.call-start = ((), (), s32[]{:S(2)}) async-start(), calls=%async_computation.1 | async-start | bytes 1605632 | tf_op jit(solution)/shard_map/psum | solution.py:73
  17.8 1.9 copy-start.4
  19.8 5.2 %copy-start.5 = (f32[1,1664]{1,0:T(1,128)S(1)}, f32[1,1664]{1,0:T(1,128)}, u32[]{:S(2)}) copy-start(f32[1,1664]{1,0:T(1,128)} %param.6) | copy-start | bytes 19972
  19.8 5.3 %copy-start.1 = (bf16[784,1664]{1,0:T(8,128)(2,1)S(1)}, bf16[784,1664]{1,0:T(8,128)(2,1)}, u32[]{:S(2)}) copy-start(bf16[784,1664]{1,0:T(8,128)(2,1)} %sub.60) | copy-start | bytes 7827460
  25.1 2.7 copy-start.2
  99.4 1.1 copy-start.3
  105.5 250.2 %all-reduce.7.cloned.1.call-start = ((), (), s32[]{:S(2)}) async-start(), calls=%async_computation.2 | async-start | bytes 6815744
  160.2 0.7 copy-start.6
  160.3 1.9 copy-start
Sparse Core Ops, SparseCore 0:
  11.3 82.5 all-gather.1
  105.6 44.4 all-reduce.4
  160.4 195.1 all-reduce.6
where the time goes:
time: 365 us; the launch traced here: 364 us
  waiting for transfers between devices  174 us (48%)
  blocking collectives  127 us (35%)
  local copies, waits for them, and re-layouts  20.9 us (6%)
  other arithmetic  15 us (4%)
  between operations  14.5 us (4%)
  matrix products  11.5 us (3%)
    unnamed x1, blocking collectives  127 us
    unnamed x4, waiting for transfers between devices  65.4 us
    all_gather x1, waiting for transfers between devices, per_device(): lax.all_gather(references, 'img', axis=1, tiled=True)[0]  64.4 us
    psum x1, waiting for transfers between devices, combine_bands(): total = lax.psum(partial_score, 'band')  44.4 us
  transfers between devices with their start and end apart: 3, of which 3 were waited for; matrix products, arithmetic and copies ran while one was open for 6% of the time, Pallas kernels for 0%

commit v1 on v0

v1 whole, which is shorter than its diff:
```python
import functools
import math

import jax
import jax.numpy as jnp
import numpy as np
from jax import lax
from jax.experimental import pallas as pl
from jax.experimental.pallas import tpu as pltpu
from jax.sharding import PartitionSpec as P

BOX = 256
SIDE = 7
HALF = SIDE // 2
PENALTY = 10000.0
BANDS = 4
COEF = 1664
TILES = COEF // 128
SPLIT = 7
PACK = SPLIT * 128
MASKW = 512
BLOCK = 2 * COEF + MASKW
ROWS = 32 * SIDE
F32 = jnp.float32
BF16 = jnp.bfloat16


def trig_tables():
    index = np.arange(COEF)
    out = np.zeros((2 * BANDS, 8, COEF), np.float32)
    for band in range(BANDS):
        freqs = ((37 * index + 11 * band) % 257 - 128, (61 * index + 29 * band) % 129)
        for axis, freq in enumerate(freqs):
            for d in range(1, HALF + 1):
                angle = ((d * freq) % BOX) * (2.0 * math.pi / BOX)
                out[4 * axis + band, 2 * d - 2] = np.cos(angle)
                out[4 * axis + band, 2 * d - 1] = np.sin(angle)
    return out


def mod(a, n):
    return lax.rem(a + 4 * n, n)


def remote(src, dst, send, recv, device):
    return pltpu.make_async_remote_copy(
        src_ref=src,
        dst_ref=dst,
        send_sem=send,
        recv_sem=recv,
        device_id=device,
        device_id_type=pl.DeviceIdType.MESH,
    )


def nt_dot(a, b):
    return lax.dot_general(a, b, (((1,), (1,)), ((), ())), preferred_element_type=F32)


def kernel(
    images_ref, refs_ref, noise_ref, masks_ref, tab_hbm,
    out_ref, tot_ref,
    tab, stage, mcat, imgbuf, wpack, rbuf, xbuf, wbuf, sbuf, post, zbuf, obuf, cbuf, fbuf,
    tab_sem, tsend, trecv, rsend, rrecv, lsend, lrecv, wsend, wrecv, fsend, frecv,
    zsend, zrecv, csend, crecv, osend, orecv,
):
    y = lax.axis_index("band")
    m = lax.axis_index("img")
    core = lax.rem(m, 2)
    x = lax.rem(m // 2, 4)
    z = m // 8

    def dev(y, z, x, c):
        return (y, (z * 4 + x) * 2 + c)

    to_y = lax.rem(z, 4)
    to_z = mod(z + mod(y - to_y + 1, 4) - 1, 8)
    my_band = lax.rem(z, 4)

    def origin(slot):
        return mod(slot - (mod(lax.rem(slot, 4) - y + 1, 4) - 1), 8)

    moved = to_y != y
    target = dev(to_y, to_z, x, core)
    source = dev(my_band, origin(z), x, core)
    partner = dev(y, z, x, 1 - core)
    zright = dev(y, mod(z + 1, 8), x, core)
    zleft = dev(y, mod(z - 1, 8), x, core)

    def plane(k):
        return mod(y + k // 4, 4), mod(x + lax.rem(k, 4), 4)

    def plane_from(k):
        return mod(y - k // 4, 4), mod(x - lax.rem(k, 4), 4)

    barrier = pltpu.get_barrier_semaphore()

    def signal(device):
        pl.semaphore_signal(barrier, inc=1, device_id=device, device_id_type=pl.DeviceIdType.MESH)

    tab_copy = pltpu.make_async_copy(tab_hbm, tab, tab_sem)
    tab_copy.start()

    @pl.when(moved)
    def _():
        signal(target)

    apart = mod(y - to_y, 4) == 2

    @pl.when(apart)
    def _():
        signal(source)

    signal(partner)

    @pl.loop(1, 8)
    def _(d):
        signal(dev(y, mod(z + d, 8), x, core))

    @pl.loop(1, 16)
    def _(k):
        py, px = plane(k)
        signal(dev(py, z, px, core))

    mcat[...] = jnp.zeros_like(mcat)
    for s in range(SIDE * SIDE):
        dx, dy = s // SIDE, s % SIDE
        mcat[2 * dx : 2 * dx + 2, dy * 64 : dy * 64 + 64] = masks_ref[s].astype(F32)
    stage[:, : 2 * COEF] = images_ref[...]
    stage[:, 2 * COEF :] = mcat[...].astype(BF16)

    values = refs_ref[...].astype(F32)
    weight = noise_ref[...]
    re, im = values[:, :COEF], values[:, COEF:]
    wre, wim = re * weight, im * weight
    norm = jnp.sum(re * wre + im * wim, axis=1, keepdims=True)
    hi = norm.astype(BF16).astype(F32)
    mid = (norm - hi).astype(BF16).astype(F32)
    low = norm - hi - mid
    lane4 = lax.broadcasted_iota(jnp.int32, (4, 128), 1)
    spare = jnp.where(lane4 == 0, hi, jnp.where(lane4 == 1, mid, jnp.where(lane4 == 2, low, 0.0)))
    wpack[0:4, :] = wre[:, :PACK]
    wpack[4:8, :] = wim[:, :PACK]
    wpack[8:12, : COEF - PACK] = wre[:, PACK:]
    wpack[12:16, : COEF - PACK] = wim[:, PACK:]
    wpack[8:12, COEF - PACK :] = spare
    wpack[12:16, COEF - PACK :] = jnp.zeros((4, 128), F32)
    rbuf[y, x, core] = wpack[...].astype(BF16)

    pl.semaphore_wait(barrier, 23 + moved.astype(jnp.int32) + apart.astype(jnp.int32))

    @pl.when(moved)
    def _():
        remote(stage, imgbuf.at[to_z], tsend, trecv, target).start()

    @pl.when(jnp.logical_not(moved))
    def _():
        imgbuf[z] = stage[...]

    def refs_copy(k):
        py, px = plane(k)
        return remote(rbuf.at[y, x, core], rbuf.at[y, x, core], wsend.at[k], wrecv.at[k], dev(py, z, px, core))

    def refs_arrival(k):
        py, px = plane_from(k)
        return remote(rbuf.at[py, px, core], rbuf.at[py, px, core], wsend.at[k], wrecv.at[k], dev(py, z, px, core))

    def refs_forward(k):
        py, px = plane_from(k)
        return remote(rbuf.at[py, px, core], rbuf.at[py, px, core], fsend.at[k], frecv.at[k], partner)

    def refs_forwarded(k):
        py, px = plane_from(k)
        return remote(rbuf.at[py, px, 1 - core], rbuf.at[py, px, 1 - core], fsend.at[k], frecv.at[k], partner)

    @pl.loop(1, 16)
    def _(k):
        refs_copy(k).start()

    refs_forward(0).start()

    @pl.when(moved)
    def _():
        remote(stage, imgbuf.at[z], tsend, trecv, source).wait_recv()

    def ring_right(step):
        slot = mod(z - (step - 1), 8)
        ref = imgbuf.at[slot] if step < 4 else imgbuf.at[slot, :, pl.ds(0, BLOCK // 2)]
        return remote(ref, ref, rsend.at[step - 1], rrecv.at[step - 1], zright)

    def ring_left(step):
        slot = mod(z + (step - 1), 8)
        ref = imgbuf.at[slot] if step < 4 else imgbuf.at[slot, :, pl.ds(BLOCK // 2, BLOCK // 2)]
        return remote(ref, ref, lsend.at[step - 1], lrecv.at[step - 1], zleft)

    def ring_arrive(step):
        slot = mod(z - step, 8)
        ref = imgbuf.at[slot] if step < 4 else imgbuf.at[slot, :, pl.ds(0, BLOCK // 2)]
        remote(ref, ref, rsend.at[step - 1], rrecv.at[step - 1], zright).wait_recv()
        slot = mod(z + step, 8)
        ref = imgbuf.at[slot] if step < 4 else imgbuf.at[slot, :, pl.ds(BLOCK // 2, BLOCK // 2)]
        remote(ref, ref, lsend.at[step - 1], lrecv.at[step - 1], zleft).wait_recv()

    def ring_start(step):
        ring_right(step).start()
        ring_left(step).start()

    ring_start(1)
    tab_copy.wait()

    def shifted(re, im, table, d):
        c, s = table[2 * d - 2 : 2 * d - 1], table[2 * d - 1 : 2 * d]
        a, b, g, h = re * c, im * s, re * s, im * c
        return (a - b, g + h), (a + b, h - g)

    def prepare_images(slot):
        band = lax.rem(slot, 4)
        first = (origin(slot) // 4) * 16

        def rows(n):
            return pl.ds(pl.multiple_of((HALF + n) * 32 + first, 16), 16)

        @pl.loop(0, TILES)
        def _(t):
            lanes = pl.ds(pl.multiple_of(t * 128, 128), 128)
            lanes_im = pl.ds(pl.multiple_of(t * 128 + COEF, 128), 128)
            out_re = pl.ds(pl.multiple_of(t * 256, 128), 128)
            out_im = pl.ds(pl.multiple_of(t * 256 + 128, 128), 128)
            raw_re, raw_im = imgbuf[slot, :, lanes], imgbuf[slot, :, lanes_im]
            xbuf[band, rows(0), out_re] = raw_re
            xbuf[band, rows(0), out_im] = raw_im
            re, im = raw_re.astype(F32), raw_im.astype(F32)
            table = tab[band, :, lanes]
            for d in range(1, HALF + 1):
                up, down = shifted(re, im, table, d)
                xbuf[band, rows(d), out_re] = up[0].astype(BF16)
                xbuf[band, rows(d), out_im] = up[1].astype(BF16)
                xbuf[band, rows(-d), out_re] = down[0].astype(BF16)
                xbuf[band, rows(-d), out_im] = down[1].astype(BF16)

    def prepare_refs(band):
        def store(t, re, im):
            lanes = pl.ds(pl.multiple_of(t * 128, 128), 128)
            out_re = pl.ds(pl.multiple_of(t * 256, 128), 128)
            out_im = pl.ds(pl.multiple_of(t * 256 + 128, 128), 128)
            table = tab[BANDS + band, :, lanes]

            def put(n, pair):
                wbuf[band, (HALF + n) * 32 : (HALF + n) * 32 + 32, out_re] = pair[0].astype(BF16)
                wbuf[band, (HALF + n) * 32 : (HALF + n) * 32 + 32, out_im] = pair[1].astype(BF16)

            put(0, (re, im))
            for d in range(1, HALF + 1):
                up, down = shifted(re, im, table, d)
                put(-d, up)
                put(d, down)

        def load(t):
            lanes = pl.ds(pl.multiple_of(t * 128, 128), 128)
            blocks = [rbuf[band, xx, cc, :, lanes].astype(F32) for xx in range(4) for cc in range(2)]
            return [jnp.concatenate([b[4 * q : 4 * q + 4] for b in blocks], axis=0) for q in range(4)]

        @pl.loop(0, SPLIT - 1)
        def _(t):
            re, im, re2, im2 = load(t)
            store(t, re, im)
            store(t + SPLIT, re2, im2)

        re, im, spare, _ = load(SPLIT - 1)
        store(SPLIT - 1, re, im)
        return spare

    def score_band(band, first):
        term = nt_dot(xbuf[band], wbuf[band])
        if first:
            sbuf[...] = term
        else:
            sbuf[...] += term

    prepare_images(z)
    ring_arrive(1)
    ring_start(2)

    @pl.loop(1, 16)
    def _(k):
        refs_arrival(k).wait_recv()
        refs_forward(k).start()

    prepare_images(mod(z - 1, 8))
    prepare_images(mod(z + 1, 8))

    ring_arrive(2)
    ring_start(3)

    @pl.loop(0, 16)
    def _(k):
        refs_forwarded(k).wait_recv()

    half = jnp.where(lax.broadcasted_iota(jnp.int32, (8, 128), 1) < 3, -0.5, 0.0).astype(BF16)
    norms = jnp.zeros((8, 32), F32)
    for band in range(BANDS):
        norms += nt_dot(half, prepare_refs(band).astype(BF16))
    norms = jnp.concatenate([norms] * SIDE, axis=1)

    prepare_images(mod(z - 2, 8))
    prepare_images(mod(z + 2, 8))
    score_band(mod(z + 2, 4), True)

    ring_arrive(3)
    ring_start(4)
    prepare_images(mod(z - 3, 8))
    prepare_images(mod(z + 3, 8))
    score_band(mod(z + 1, 4), False)
    score_band(mod(z + 3, 4), False)
    row = lax.broadcasted_iota(jnp.int32, (MASKW, ROWS), 0)
    lane = lax.broadcasted_iota(jnp.int32, (MASKW, ROWS), 1)
    spread = jnp.where(row == (lane >> 5) * 64 + 8 * z + ((lane & 31) >> 2), 1.0, 0.0).astype(BF16)

    ring_arrive(4)
    prepare_images(mod(z + 4, 8))
    score_band(lax.rem(z, 4), False)

    kept = []
    for e in range(2):
        total = jnp.zeros((16, MASKW), F32)
        for band in range(BANDS):
            slot = mod(y + 4 * e + mod(band - y + 1, 4) - 1, 8)
            total += imgbuf[slot, :, 2 * COEF :].astype(F32)
        kept.append(lax.dot_general(total.astype(BF16), spread, (((1,), (0,)), ((), ())), preferred_element_type=F32))

    lane8 = lax.broadcasted_iota(jnp.int32, (8, 128), 1)
    message = jnp.zeros((8, 128), F32)
    for q in range(4):
        e, block = q // 2, q % 2
        tiles = []
        for dx in range(SIDE):
            line = kept[e][2 * dx + block : 2 * dx + block + 1]
            tiles.append(sbuf[dx * 32 + q * 8 : dx * 32 + q * 8 + 8, :] + norms - PENALTY * (BANDS - line))
        peak = tiles[0]
        for tile in tiles[1:]:
            peak = jnp.maximum(peak, tile)
        peak = jnp.max(peak, axis=1, keepdims=True)
        mass = jnp.zeros((8, ROWS), F32)
        for dx in range(SIDE):
            raised = jnp.exp(tiles[dx] - peak)
            sbuf[dx * 32 + q * 8 : dx * 32 + q * 8 + 8, :] = raised
            mass += raised
        mass = jnp.sum(mass, axis=1, keepdims=True)
        message = jnp.where(lane8 == q, peak, jnp.where(lane8 == 4 + q, mass, message))
    zbuf[z] = message

    def z_copy(d):
        return remote(zbuf.at[z], zbuf.at[z], zsend.at[d], zrecv.at[d], dev(y, mod(z + d, 8), x, core))

    def z_arrival(d):
        slot = mod(z - d, 8)
        return remote(zbuf.at[slot], zbuf.at[slot], zsend.at[d], zrecv.at[d], dev(y, slot, x, core))

    @pl.loop(1, 8)
    def _(d):
        z_copy(d).start()

    @pl.loop(1, 8)
    def _(d):
        z_arrival(d).wait_recv()

    top = zbuf[0]
    for slot in range(1, 8):
        top = jnp.maximum(top, zbuf[slot])
    whole = jnp.zeros((8, 128), F32)
    for slot in range(8):
        part = zbuf[slot]
        whole += pltpu.roll(part, 124, 1) * jnp.exp(jnp.where(lane8 < 4, part - top, 0.0))
    factor = jnp.exp(jnp.where(lane8 < 4, message - top, 0.0)) / jnp.where(lane8 < 4, whole, 1.0)
    for q in range(4):
        scale = factor[:, q : q + 1]
        for dx in range(SIDE):
            sbuf[dx * 32 + q * 8 : dx * 32 + q * 8 + 8, :] = sbuf[dx * 32 + q * 8 : dx * 32 + q * 8 + 8, :] * scale
    prob = sbuf[...].T
    post[...] = prob.astype(BF16)
    mass = jnp.sum(prob, axis=1, keepdims=True)
    totals = mass[0:32]
    for dy in range(1, SIDE):
        totals += mass[dy * 32 : dy * 32 + 32]
    thi = totals.astype(BF16).astype(F32)
    lane32 = lax.broadcasted_iota(jnp.int32, (32, 128), 1)
    spare_re = jnp.where(lane32 == 0, thi, jnp.where(lane32 == 1, totals - thi, 0.0))
    spare_im = jnp.zeros((32, 128), F32)

    def sums_tile(band, t):
        lanes = pl.ds(pl.multiple_of(t * 128, 128), 128)
        both = pl.ds(pl.multiple_of(t * 256, 256), 256)
        g = jnp.dot(post[...], xbuf[band, :, both], preferred_element_type=F32)
        table = tab[BANDS + band, :, lanes]

        def part(n):
            r = (HALF + n) * 32
            return g[r : r + 32, :128], g[r : r + 32, 128:]

        re, im = part(0)
        for d in range(1, HALF + 1):
            c, s = table[2 * d - 2 : 2 * d - 1], table[2 * d - 1 : 2 * d]
            (ur, ui), (dr, di) = part(d), part(-d)
            re = re + c * (ur + dr) - s * (ui - di)
            im = im + s * (ur - dr) + c * (ui + di)
        return re, im

    def pack(band, t, upper, lower):
        lanes = pl.ds(pl.multiple_of(t * 128, 128), 128)
        for xx in range(4):
            for cc in range(2):
                r = xx * 8 + cc * 4
                rows = jnp.concatenate([a[r : r + 4] for a in (*upper, *lower)], axis=0)
                obuf[band, cc, xx, :, lanes] = rows.astype(BF16)

    def core_copy(k):
        band = mod(y + k, 4)
        return remote(obuf.at[band, 1 - core], cbuf.at[k], csend.at[k], crecv.at[k], partner)

    def out_copy(k):
        py, px = plane(k)
        return remote(obuf.at[py, core, px], fbuf.at[k], osend.at[k], orecv.at[k], dev(py, z, px, core))

    def sums_band(k):
        band = mod(y + k, 4)

        @pl.loop(0, SPLIT - 1)
        def _(t):
            pack(band, t, sums_tile(band, t), sums_tile(band, t + SPLIT))

        pack(band, SPLIT - 1, sums_tile(band, SPLIT - 1), (spare_re, spare_im))
        core_copy(k).start()

    def owners_band(k):
        band = mod(y + k, 4)
        core_copy(k).wait_recv()
        for xx in range(4):
            mine = obuf[band, core, xx].astype(F32) + cbuf[k, xx].astype(F32)
            obuf[band, core, xx] = mine.astype(BF16)
        for j in range(4):
            if (4 * k + j) % 16:
                out_copy(4 * k + j).start()

    sums_band(1)
    sums_band(2)
    owners_band(1)
    sums_band(3)
    owners_band(2)
    sums_band(0)
    owners_band(3)
    owners_band(0)

    @pl.loop(1, 16)
    def _(k):
        out_copy(k).wait_recv()

    final = obuf[y, core, x].astype(F32)
    for k in range(1, 16):
        final += fbuf[k].astype(F32)
    out_ref[:, :PACK] = final[0:4]
    out_ref[:, COEF : COEF + PACK] = final[4:8]
    out_ref[:, PACK:COEF] = final[8:12, : COEF - PACK]
    out_ref[:, COEF + PACK :] = final[12:16, : COEF - PACK]
    pair = final[8:12, COEF - PACK : COEF - PACK + 1] + final[8:12, COEF - PACK + 1 : COEF - PACK + 2]
    eye = lax.broadcasted_iota(jnp.int32, (4, 4), 0) == lax.broadcasted_iota(jnp.int32, (4, 4), 1)
    tot_ref[...] = jnp.sum(jnp.where(eye, pair, 0.0), axis=0, keepdims=True)

    @pl.when(moved)
    def _():
        remote(stage, imgbuf.at[to_z], tsend, trecv, target).wait_send()

    for step in range(1, 5):
        ring_right(step).wait_send()
        ring_left(step).wait_send()

    @pl.loop(1, 16)
    def _(k):
        refs_copy(k).wait_send()
        out_copy(k).wait_send()

    @pl.loop(0, 16)
    def _(k):
        refs_forward(k).wait_send()

    @pl.loop(1, 8)
    def _(d):
        z_copy(d).wait_send()

    @pl.loop(0, 4)
    def _(k):
        core_copy(k).wait_send()


def per_device(images, references, noise_weight, masks):
    vmem = pl.BlockSpec(memory_space=pltpu.VMEM)
    dma = pltpu.SemaphoreType.DMA
    sums, totals = pl.pallas_call(
        kernel,
        out_shape=(jax.ShapeDtypeStruct((4, 2 * COEF), F32), jax.ShapeDtypeStruct((1, 4), F32)),
        in_specs=[vmem, vmem, vmem, vmem, pl.BlockSpec(memory_space=pl.ANY)],
        out_specs=(vmem, vmem),
        scratch_shapes=[
            pltpu.VMEM((2 * BANDS, 8, COEF), F32),
            pltpu.VMEM((16, BLOCK), BF16),
            pltpu.VMEM((16, MASKW), F32),
            pltpu.VMEM((8, 16, BLOCK), BF16),
            pltpu.VMEM((16, PACK), F32),
            pltpu.VMEM((BANDS, 4, 2, 16, PACK), BF16),
            pltpu.VMEM((BANDS, ROWS, 2 * COEF), BF16),
            pltpu.VMEM((BANDS, ROWS, 2 * COEF), BF16),
            pltpu.VMEM((ROWS, ROWS), F32),
            pltpu.VMEM((ROWS, ROWS), BF16),
            pltpu.VMEM((8, 8, 128), F32),
            pltpu.VMEM((BANDS, 2, 4, 16, PACK), BF16),
            pltpu.VMEM((BANDS, 4, 16, PACK), BF16),
            pltpu.VMEM((16, 16, PACK), BF16),
            dma, dma, dma,
            dma((4,)), dma((4,)), dma((4,)), dma((4,)),
            dma((16,)), dma((16,)), dma((16,)), dma((16,)),
            dma((8,)), dma((8,)), dma((4,)), dma((4,)), dma((16,)), dma((16,)),
        ],
        compiler_params=pltpu.CompilerParams(
            collective_id=0, has_side_effects=True, vmem_limit_bytes=48 * 1024 * 1024
        ),
    )(
        images[0],
        references[0],
        noise_weight,
        jnp.transpose(masks[0], (2, 0, 1)),
        jnp.asarray(trig_tables()),
    )
    return sums[None], totals[0]


def solution(mesh):
    in_specs = (
        P("band", "img", None),
        P("band", "img", None),
        P("band", None),
        P("band", "img", None, None),
    )
    out_specs = (P("band", "img", None), P("img"))
    return jax.shard_map(
        per_device, mesh=mesh, in_specs=in_specs, out_specs=out_specs, check_vma=False
    )
```

time: 365 us -> 68 us (0.19)
  waiting for transfers between devices: 174 us -> 0 us
  blocking collectives: 127 us -> 0 us
  Pallas kernels: 0 us -> 61.8 us
  local copies, waits for them, and re-layouts: 20.9 us -> 5.27 us
  other arithmetic: 15 us -> 0 us
  between operations: 14.5 us -> 0.65 us
  matrix products: 11.5 us -> 0 us
    unnamed x1 -> x0, blocking collectives: 127 us -> none
    unnamed x4 -> x0, waiting for transfers between devices: 65.4 us -> none
    all_gather x1 -> x0, waiting for transfers between devices: 64.4 us -> none  [per_device(): lax.all_gather(references, 'img', axis=1, tiled=True)[0]]
    pallas_call x0 -> x1, Pallas kernels: none -> 61.8 us  [per_device(): pl.pallas_call(kernel, out_shape=(jax.ShapeDtypeStruct((4, 2 * COEF), F32...]
    psum x1 -> x0, waiting for transfers between devices: 44.4 us -> none  [combine_bands(): total = lax.psum(partial_score, 'band')]
    dot_general x2 -> x0, matrix products: 11.5 us -> none  [the longest x1 6.59 us: per_device(): lax.dot_general(post, aligned, (((0,), (0,)), ((), ())), preferred_elemen...]
    convert_element_type x2 -> x0, other arithmetic: 6.32 us -> none  [the longest x1 5.47 us: prepare(): values = projections.astype(jnp.float32)]
    reshape x2 -> x0, local copies, waits for them, and re-layouts: 3.73 us -> none  [penalty(): dropped.reshape(blocks * img_block * shift_count, owners * orient_dev)]
  transfers between devices with their start and end apart: 3 -> 0, of which waited for: 3 -> 0; matrix products, arithmetic and copies ran while one was open for 6% -> 0% of each run, Pallas kernels for 0% -> 0%
where the time goes in v1:
time: 68 us; the launch traced here: 67.7 us
  Pallas kernels  61.8 us (91%)
  local copies, waits for them, and re-layouts  5.27 us (8%)
    pallas_call x1, Pallas kernels, per_device(): pl.pallas_call(kernel, out_shape=(jax.ShapeDtypeStruct((4, 2 * COEF), F32...  61.8 us
    unnamed x12, local copies, waits for them, and re-layouts  5.27 us

profile of v1, /device:TPU:1, one launch (start us, length us, event | category | flops | bytes accessed | tf_op | source)
XLA Modules:
  0.0 67.7 jit_solution(8950557854223909370)
XLA Ops:
  0.6 0.0 copy-start
  0.6 1.0 %copy-done = f32[8,8,1664]{2,1,0:T(8,128)S(1)} copy-done((f32[8,8,1664]{2,1,0:T(8,128)S(1)}, f32[8,8,1664]{2,1,0:T(8,128)}, u32[]{:S(2)}) %copy-start) | copy-done | bytes 426008
  1.6 0.0 copy-start.1
  1.6 0.9 %copy-done.1 = bf16[1,16,3328]{2,1,0:T(8,128)(2,1)S(1)} copy-done((bf16[1,16,3328]{2,1,0:T(8,128)(2,1)S(1)}, bf16[1,16,3328]{2,1,0:T(8,128)(2,1)}, u32[]{:S(2)}) %copy-start.1) | copy-done | bytes 106520
  2.5 0.0 copy-start.2
  2.5 0.8 %copy-done.2 = s32[1,2,64,49]{2,1,3,0:T(2,128)S(1)} copy-done((s32[1,2,64,49]{2,1,3,0:T(2,128)S(1)}, s32[1,2,64,49]{2,1,3,0:T(2,128)}, u32[]{:S(2)}) %copy-start.2) | copy-done | bytes 25112
  3.3 0.0 copy-start.3
  3.3 0.7 %copy-done.3 = bf16[1,4,3328]{2,1,0:T(4,128)(2,1)S(1)} copy-done((bf16[1,4,3328]{2,1,0:T(4,128)(2,1)S(1)}, bf16[1,4,3328]{2,1,0:T(4,128)(2,1)}, u32[]{:S(2)}) %copy-start.3) | copy-done | bytes 26648
  4.1 0.0 copy-start.4
  4.1 0.7 %copy-done.4 = f32[1,1664]{1,0:T(1,128)S(1)} copy-done((f32[1,1664]{1,0:T(1,128)S(1)}, f32[1,1664]{1,0:T(1,128)}, u32[]{:S(2)}) %copy-start.4) | copy-done | bytes 6680
  4.8 61.8 %shard_map.68 = (f32[4,3328]{1,0:T(4,128)S(1)}, f32[1,4]{1,0:T(1,128)S(1)}) custom-call(bf16[16,3328]{1,0:T(8,128)(2,1)S(1)} %bitcast.7, bf16[4,3328]{1,0:T(4,128)(2,1)S(1)} %bitcast.10, f32[1,1664]{1,0:T(1,128)S(1)} %copy-done.4, s32[49,2,64]{2,1,0:T(2,128)S(1)} %bitcast.9, f32[8,8,1664]{2,1,0:T(8,128)S(1)} %copy-done), custom_call_target="tpu_custom_call" | custom-call | tf_op jit(solution)/shard_map/pallas_call | solution.py:497
  66.6 0.6 copy.9
  67.2 0.5 copy.10
Async XLA Ops:
  0.6 1.0 %copy-start = (f32[8,8,1664]{2,1,0:T(8,128)S(1)}, f32[8,8,1664]{2,1,0:T(8,128)}, u32[]{:S(2)}) copy-start(f32[8,8,1664]{2,1,0:T(8,128)} %constant.2.clone.tab_hbm) | copy-start | bytes 1277956
  1.6 0.9 %copy-start.1 = (bf16[1,16,3328]{2,1,0:T(8,128)(2,1)S(1)}, bf16[1,16,3328]{2,1,0:T(8,128)(2,1)}, u32[]{:S(2)}) copy-start(bf16[1,16,3328]{2,1,0:T(8,128)(2,1)} %param.5) | copy-start | bytes 319492
  2.5 0.8 %copy-start.2 = (s32[1,2,64,49]{2,1,3,0:T(2,128)S(1)}, s32[1,2,64,49]{2,1,3,0:T(2,128)}, u32[]{:S(2)}) copy-start(s32[1,2,64,49]{2,1,3,0:T(2,128)} %param.8) | copy-start | bytes 75268
  3.3 0.7 %copy-start.3 = (bf16[1,4,3328]{2,1,0:T(4,128)(2,1)S(1)}, bf16[1,4,3328]{2,1,0:T(4,128)(2,1)}, u32[]{:S(2)}) copy-start(bf16[1,4,3328]{2,1,0:T(4,128)(2,1)} %param.6) | copy-start | bytes 79876
  4.1 0.7 %copy-start.4 = (f32[1,1664]{1,0:T(1,128)S(1)}, f32[1,1664]{1,0:T(1,128)}, u32[]{:S(2)}) copy-start(f32[1,1664]{1,0:T(1,128)} %noise_ref.1) | copy-start | bytes 19972

commit v2 on v1

--- a/solution.py
+++ b/solution.py
@@ -20,6 +20,7 @@
 PACK = SPLIT * 128
 MASKW = 512
 BLOCK = 2 * COEF + MASKW
+CHUNKS = ((0, 8), (8, 8), (16, 7), (23, 7))
 ROWS = 32 * SIDE
 F32 = jnp.float32
 BF16 = jnp.bfloat16
@@ -58,10 +59,10 @@
 
 
 def kernel(
-    images_ref, refs_ref, noise_ref, masks_ref, tab_hbm,
+    images_hbm, refs_hbm, noise_hbm, masks_hbm, tab_hbm,
     out_ref, tot_ref,
-    tab, stage, mcat, imgbuf, wpack, rbuf, xbuf, wbuf, sbuf, post, zbuf, obuf, cbuf, fbuf,
-    tab_sem, tsend, trecv, rsend, rrecv, lsend, lrecv, wsend, wrecv, fsend, frecv,
+    refs_ref, noise_ref, masks_ref, tab, stage, mcat, imgbuf, wpack, rbuf, xbuf, wbuf, sbuf, post, zbuf, obuf, cbuf, fbuf,
+    in_sem, tab_sem, tsend, trecv, rsend, rrecv, lsend, lrecv, wsend, wrecv, fsend, frecv,
     zsend, zrecv, csend, crecv, osend, orecv,
 ):
     y = lax.axis_index("band")
@@ -98,6 +99,13 @@
     def signal(device):
         pl.semaphore_signal(barrier, inc=1, device_id=device, device_id_type=pl.DeviceIdType.MESH)
 
+    inputs = [
+        pltpu.make_async_copy(refs_hbm, refs_ref, in_sem.at[0]),
+        pltpu.make_async_copy(noise_hbm, noise_ref, in_sem.at[1]),
+        pltpu.make_async_copy(masks_hbm, masks_ref, in_sem.at[2]),
+    ]
+    for copy in inputs:
+        copy.start()
     tab_copy = pltpu.make_async_copy(tab_hbm, tab, tab_sem)
     tab_copy.start()
 
@@ -122,12 +130,13 @@
         py, px = plane(k)
         signal(dev(py, z, px, core))
 
+    for copy in inputs:
+        copy.wait()
     mcat[...] = jnp.zeros_like(mcat)
     for s in range(SIDE * SIDE):
         dx, dy = s // SIDE, s % SIDE
         mcat[2 * dx : 2 * dx + 2, dy * 64 : dy * 64 + 64] = masks_ref[s].astype(F32)
-    stage[:, : 2 * COEF] = images_ref[...]
-    stage[:, 2 * COEF :] = mcat[...].astype(BF16)
+    stage[...] = mcat[...].astype(BF16)
 
     values = refs_ref[...].astype(F32)
     weight = noise_ref[...]
@@ -149,13 +158,34 @@
 
     pl.semaphore_wait(barrier, 23 + moved.astype(jnp.int32) + apart.astype(jnp.int32))
 
+    def lanes_of(j):
+        return pl.ds(CHUNKS[j][0] * 128, CHUNKS[j][1] * 128)
+
+    def piece(j, slot):
+        if j == 4:
+            return stage, imgbuf.at[slot, :, pl.ds(2 * COEF, MASKW)]
+        first = CHUNKS[j][0] * 128
+        lanes = pl.ds(first, min(CHUNKS[j][1] * 128, 2 * COEF - first))
+        return images_hbm.at[:, lanes], imgbuf.at[slot, :, lanes]
+
+    def move(j):
+        return remote(*piece(j, to_z), tsend.at[j], trecv.at[j], target)
+
+    def moved_in(j):
+        return remote(*piece(j, z), tsend.at[j], trecv.at[j], source)
+
+    def keep(j):
+        return pltpu.make_async_copy(*piece(j, z), tsend.at[j])
+
     @pl.when(moved)
     def _():
-        remote(stage, imgbuf.at[to_z], tsend, trecv, target).start()
+        for j in range(5):
+            move(j).start()
 
     @pl.when(jnp.logical_not(moved))
     def _():
-        imgbuf[z] = stage[...]
+        for j in range(5):
+            keep(j).start()
 
     def refs_copy(k):
         py, px = plane(k)
@@ -179,33 +209,43 @@
 
     refs_forward(0).start()
 
-    @pl.when(moved)
-    def _():
-        remote(stage, imgbuf.at[z], tsend, trecv, source).wait_recv()
-
-    def ring_right(step):
-        slot = mod(z - (step - 1), 8)
-        ref = imgbuf.at[slot] if step < 4 else imgbuf.at[slot, :, pl.ds(0, BLOCK // 2)]
-        return remote(ref, ref, rsend.at[step - 1], rrecv.at[step - 1], zright)
-
-    def ring_left(step):
-        slot = mod(z + (step - 1), 8)
-        ref = imgbuf.at[slot] if step < 4 else imgbuf.at[slot, :, pl.ds(BLOCK // 2, BLOCK // 2)]
-        return remote(ref, ref, lsend.at[step - 1], lrecv.at[step - 1], zleft)
-
-    def ring_arrive(step):
-        slot = mod(z - step, 8)
-        ref = imgbuf.at[slot] if step < 4 else imgbuf.at[slot, :, pl.ds(0, BLOCK // 2)]
-        remote(ref, ref, rsend.at[step - 1], rrecv.at[step - 1], zright).wait_recv()
-        slot = mod(z + step, 8)
-        ref = imgbuf.at[slot] if step < 4 else imgbuf.at[slot, :, pl.ds(BLOCK // 2, BLOCK // 2)]
-        remote(ref, ref, lsend.at[step - 1], lrecv.at[step - 1], zleft).wait_recv()
-
-    def ring_start(step):
-        ring_right(step).start()
-        ring_left(step).start()
-
-    ring_start(1)
+    RIGHT = [(0, 1, 2, 3)] * 3 + [(0, 1)]
+    LEFT = [(0, 1, 2, 3)] * 3 + [(2, 3)]
+
+    def ring_copy(slot, step, j, send, recv, device):
+        ref = imgbuf.at[slot, :, lanes_of(j)]
+        return remote(ref, ref, send.at[step - 1, j], recv.at[step - 1, j], device)
+
+    def ring_right(step, j):
+        return ring_copy(mod(z - (step - 1), 8), step, j, rsend, rrecv, zright)
+
+    def ring_left(step, j):
+        return ring_copy(mod(z + (step - 1), 8), step, j, lsend, lrecv, zleft)
+
+    def ring_step(step):
+        for j in range(4):
+            if j in RIGHT[step - 1]:
+                ring_copy(mod(z - step, 8), step, j, rsend, rrecv, zleft).wait_recv()
+                if step < 4 and j in RIGHT[step]:
+                    ring_right(step + 1, j).start()
+            if j in LEFT[step - 1]:
+                ring_copy(mod(z + step, 8), step, j, lsend, lrecv, zright).wait_recv()
+                if step < 4 and j in LEFT[step]:
+                    ring_left(step + 1, j).start()
+
+    for j in range(4):
+        for jj in (3, 4) if j == 3 else (j,):
+
+            @pl.when(moved)
+            def _():
+                moved_in(jj).wait_recv()
+
+            @pl.when(jnp.logical_not(moved))
+            def _():
+                keep(jj).wait()
+
+        ring_right(1, j).start()
+        ring_left(1, j).start()
     tab_copy.wait()
 
     def shifted(re, im, table, d):
@@ -278,19 +318,18 @@
             sbuf[...] += term
 
     prepare_images(z)
-    ring_arrive(1)
-    ring_start(2)
+    ring_step(1)
+    prepare_images(mod(z - 1, 8))
+    prepare_images(mod(z + 1, 8))
 
     @pl.loop(1, 16)
     def _(k):
         refs_arrival(k).wait_recv()
         refs_forward(k).start()
 
-    prepare_images(mod(z - 1, 8))
-    prepare_images(mod(z + 1, 8))
-
-    ring_arrive(2)
-    ring_start(3)
+    ring_step(2)
+    prepare_images(mod(z - 2, 8))
+    prepare_images(mod(z + 2, 8))
 
     @pl.loop(0, 16)
     def _(k):
@@ -301,13 +340,9 @@
     for band in range(BANDS):
         norms += nt_dot(half, prepare_refs(band).astype(BF16))
     norms = jnp.concatenate([norms] * SIDE, axis=1)
-
-    prepare_images(mod(z - 2, 8))
-    prepare_images(mod(z + 2, 8))
     score_band(mod(z + 2, 4), True)
 
-    ring_arrive(3)
-    ring_start(4)
+    ring_step(3)
     prepare_images(mod(z - 3, 8))
     prepare_images(mod(z + 3, 8))
     score_band(mod(z + 1, 4), False)
@@ -316,7 +351,7 @@
     lane = lax.broadcasted_iota(jnp.int32, (MASKW, ROWS), 1)
     spread = jnp.where(row == (lane >> 5) * 64 + 8 * z + ((lane & 31) >> 2), 1.0, 0.0).astype(BF16)
 
-    ring_arrive(4)
+    ring_step(4)
     prepare_images(mod(z + 4, 8))
     score_band(lax.rem(z, 4), False)
 
@@ -467,11 +502,14 @@
 
     @pl.when(moved)
     def _():
-        remote(stage, imgbuf.at[to_z], tsend, trecv, target).wait_send()
+        for j in range(5):
+            move(j).wait_send()
 
     for step in range(1, 5):
-        ring_right(step).wait_send()
-        ring_left(step).wait_send()
+        for j in RIGHT[step - 1]:
+            ring_right(step, j).wait_send()
+        for j in LEFT[step - 1]:
+            ring_left(step, j).wait_send()
 
     @pl.loop(1, 16)
     def _(k):
@@ -497,11 +535,14 @@
     sums, totals = pl.pallas_call(
         kernel,
         out_shape=(jax.ShapeDtypeStruct((4, 2 * COEF), F32), jax.ShapeDtypeStruct((1, 4), F32)),
-        in_specs=[vmem, vmem, vmem, vmem, pl.BlockSpec(memory_space=pl.ANY)],
+        in_specs=[pl.BlockSpec(memory_space=pltpu.HBM)] * 5,
         out_specs=(vmem, vmem),
         scratch_shapes=[
+            pltpu.VMEM((4, 2 * COEF), BF16),
+            pltpu.VMEM((1, COEF), F32),
+            pltpu.VMEM((SIDE * SIDE, 2, 64), jnp.int32),
             pltpu.VMEM((2 * BANDS, 8, COEF), F32),
-            pltpu.VMEM((16, BLOCK), BF16),
+            pltpu.VMEM((16, MASKW), BF16),
             pltpu.VMEM((16, MASKW), F32),
             pltpu.VMEM((8, 16, BLOCK), BF16),
             pltpu.VMEM((16, PACK), F32),
@@ -514,13 +555,13 @@
             pltpu.VMEM((BANDS, 2, 4, 16, PACK), BF16),
             pltpu.VMEM((BANDS, 4, 16, PACK), BF16),
             pltpu.VMEM((16, 16, PACK), BF16),
-            dma, dma, dma,
-            dma((4,)), dma((4,)), dma((4,)), dma((4,)),
+            dma((3,)), dma, dma((5,)), dma((5,)),
+            dma((4, 4)), dma((4, 4)), dma((4, 4)), dma((4, 4)),
             dma((16,)), dma((16,)), dma((16,)), dma((16,)),
             dma((8,)), dma((8,)), dma((4,)), dma((4,)), dma((16,)), dma((16,)),
         ],
         compiler_params=pltpu.CompilerParams(
-            collective_id=0, has_side_effects=True, vmem_limit_bytes=48 * 1024 * 1024
+            collective_id=0, has_side_effects=True, vmem_limit_bytes=60 * 1024 * 1024
         ),
     )(
         images[0],

time: 68 us -> 61 us (0.90)
  Pallas kernels: 61.8 us -> 57.7 us
  local copies, waits for them, and re-layouts: 5.27 us -> 1.95 us
    pallas_call x1, Pallas kernels: 61.8 us -> 57.7 us  [per_device(): pl.pallas_call(kernel, out_shape=(jax.ShapeDtypeStruct((4, 2 * COEF), F32...]
    unnamed x12 -> x4, local copies, waits for them, and re-layouts: 5.27 us -> 1.95 us
where the time goes in v2:
time: 61 us; the launch traced here: 60.3 us
  Pallas kernels  57.7 us (95%)
  local copies, waits for them, and re-layouts  1.95 us (3%)
  between operations  0.65 us (1%)
    pallas_call x1, Pallas kernels, per_device(): pl.pallas_call(kernel, out_shape=(jax.ShapeDtypeStruct((4, 2 * COEF), F32...  57.7 us
    unnamed x4, local copies, waits for them, and re-layouts  1.95 us

profile of v2, /device:TPU:1, one launch (start us, length us, event | category | flops | bytes accessed | tf_op | source)
XLA Modules:
  0.0 60.3 jit_solution(17989354716293313144)
XLA Ops:
  0.6 57.7 %shard_map.68 = (f32[4,3328]{1,0:T(4,128)}, f32[1,4]{1,0:T(1,128)}) custom-call(bf16[16,3328]{1,0:T(8,128)(2,1)} %bitcast.7, bf16[4,3328]{1,0:T(4,128)(2,1)} %bitcast.10, f32[1,1664]{1,0:T(1,128)} %noise_hbm.1, s32[49,2,64]{2,1,0:T(2,128)} %bitcast.9, f32[8,8,1664]{2,1,0:T(8,128)} %constant.2.clone.tab_hbm), custom_call_target="tpu_custom_call" | custom-call | tf_op jit(solution)/shard_map/pallas_call | solution.py:535
  58.4 0.0 copy-start
  58.4 1.4 %copy.9 = f32[1,4,3328]{2,1,0:T(4,128)} copy(f32[1,4,3328]{2,1,0:T(4,128)} %bitcast.8) | data formatting | bytes 106496
  59.8 0.0 copy-done
  59.8 0.5 copy.10
Async XLA Ops:
  58.4 1.4 %copy-start = (f32[1,4]{1,0:T(1,128)S(1)}, f32[1,4]{1,0:T(1,128)}, u32[]{:S(2)}) copy-start(f32[1,4]{1,0:T(1,128)} %get-tuple-element.5) | copy-start | bytes 52

commit v3 on v2

--- a/solution.py
+++ b/solution.py
@@ -130,13 +130,63 @@
         py, px = plane(k)
         signal(dev(py, z, px, core))
 
+    pl.semaphore_wait(barrier, 23 + moved.astype(jnp.int32) + apart.astype(jnp.int32))
+
+    def lanes_of(j):
+        return pl.ds(CHUNKS[j][0] * 128, CHUNKS[j][1] * 128)
+
+    def piece(j, slot):
+        if j == 4:
+            return stage, imgbuf.at[slot, :, pl.ds(2 * COEF, MASKW)]
+        first = CHUNKS[j][0] * 128
+        lanes = pl.ds(first, min(CHUNKS[j][1] * 128, 2 * COEF - first))
+        return images_hbm.at[:, lanes], imgbuf.at[slot, :, lanes]
+
+    def move(j):
+        return remote(*piece(j, to_z), tsend.at[j], trecv.at[j], target)
+
+    def moved_in(j):
+        return remote(*piece(j, z), tsend.at[j], trecv.at[j], source)
+
+    def keep(j):
+        return pltpu.make_async_copy(*piece(j, z), tsend.at[j])
+
+    def move_start(j):
+        @pl.when(moved)
+        def _():
+            move(j).start()
+
+        @pl.when(jnp.logical_not(moved))
+        def _():
+            keep(j).start()
+
+    for j in range(4):
+        move_start(j)
+
+    def refs_copy(k):
+        py, px = plane(k)
+        return remote(rbuf.at[core, y, x], rbuf.at[core, y, x], wsend.at[k], wrecv.at[k], dev(py, z, px, core))
+
+    def refs_arrival(k):
+        py, px = plane_from(k)
+        return remote(rbuf.at[core, py, px], rbuf.at[core, py, px], wsend.at[k], wrecv.at[k], dev(py, z, px, core))
+
+    def refs_forward(g):
+        band = mod(y - g, 4)
+        return remote(rbuf.at[core, band], rbuf.at[core, band], fsend.at[g], frecv.at[g], partner)
+
+    def refs_forwarded(g):
+        band = mod(y - g, 4)
+        return remote(rbuf.at[1 - core, band], rbuf.at[1 - core, band], fsend.at[g], frecv.at[g], partner)
+
+    def refs_group(g):
+        for k in range(4 * g, 4 * g + 4):
+            if k:
+                refs_arrival(k).wait_recv()
+        refs_forward(g).start()
+
     for copy in inputs:
         copy.wait()
-    mcat[...] = jnp.zeros_like(mcat)
-    for s in range(SIDE * SIDE):
-        dx, dy = s // SIDE, s % SIDE
-        mcat[2 * dx : 2 * dx + 2, dy * 64 : dy * 64 + 64] = masks_ref[s].astype(F32)
-    stage[...] = mcat[...].astype(BF16)
 
     values = refs_ref[...].astype(F32)
     weight = noise_ref[...]
@@ -154,60 +204,18 @@
     wpack[12:16, : COEF - PACK] = wim[:, PACK:]
     wpack[8:12, COEF - PACK :] = spare
     wpack[12:16, COEF - PACK :] = jnp.zeros((4, 128), F32)
-    rbuf[y, x, core] = wpack[...].astype(BF16)
-
-    pl.semaphore_wait(barrier, 23 + moved.astype(jnp.int32) + apart.astype(jnp.int32))
-
-    def lanes_of(j):
-        return pl.ds(CHUNKS[j][0] * 128, CHUNKS[j][1] * 128)
-
-    def piece(j, slot):
-        if j == 4:
-            return stage, imgbuf.at[slot, :, pl.ds(2 * COEF, MASKW)]
-        first = CHUNKS[j][0] * 128
-        lanes = pl.ds(first, min(CHUNKS[j][1] * 128, 2 * COEF - first))
-        return images_hbm.at[:, lanes], imgbuf.at[slot, :, lanes]
-
-    def move(j):
-        return remote(*piece(j, to_z), tsend.at[j], trecv.at[j], target)
-
-    def moved_in(j):
-        return remote(*piece(j, z), tsend.at[j], trecv.at[j], source)
-
-    def keep(j):
-        return pltpu.make_async_copy(*piece(j, z), tsend.at[j])
-
-    @pl.when(moved)
-    def _():
-        for j in range(5):
-            move(j).start()
-
-    @pl.when(jnp.logical_not(moved))
-    def _():
-        for j in range(5):
-            keep(j).start()
-
-    def refs_copy(k):
-        py, px = plane(k)
-        return remote(rbuf.at[y, x, core], rbuf.at[y, x, core], wsend.at[k], wrecv.at[k], dev(py, z, px, core))
-
-    def refs_arrival(k):
-        py, px = plane_from(k)
-        return remote(rbuf.at[py, px, core], rbuf.at[py, px, core], wsend.at[k], wrecv.at[k], dev(py, z, px, core))
-
-    def refs_forward(k):
-        py, px = plane_from(k)
-        return remote(rbuf.at[py, px, core], rbuf.at[py, px, core], fsend.at[k], frecv.at[k], partner)
-
-    def refs_forwarded(k):
-        py, px = plane_from(k)
-        return remote(rbuf.at[py, px, 1 - core], rbuf.at[py, px, 1 - core], fsend.at[k], frecv.at[k], partner)
-
-    @pl.loop(1, 16)
-    def _(k):
+    rbuf[core, y, x] = wpack[...].astype(BF16)
+
+    for k in (10, 11, 14, 15, 2, 8, 9, 6, 5, 7, 13, 12, 4, 3, 1):
         refs_copy(k).start()
 
-    refs_forward(0).start()
+    mcat[...] = jnp.zeros_like(mcat)
+    for s in range(SIDE * SIDE):
+        dx, dy = s // SIDE, s % SIDE
+        mcat[2 * dx : 2 * dx + 2, dy * 64 : dy * 64 + 64] = masks_ref[s].astype(F32)
+    stage[...] = mcat[...].astype(BF16)
+
+    move_start(4)
 
     RIGHT = [(0, 1, 2, 3)] * 3 + [(0, 1)]
     LEFT = [(0, 1, 2, 3)] * 3 + [(2, 3)]
@@ -222,7 +230,7 @@
     def ring_left(step, j):
         return ring_copy(mod(z + (step - 1), 8), step, j, lsend, lrecv, zleft)
 
-    def ring_step(step):
+    def ring_step(step, *gaps):
         for j in range(4):
             if j in RIGHT[step - 1]:
                 ring_copy(mod(z - step, 8), step, j, rsend, rrecv, zleft).wait_recv()
@@ -232,6 +240,8 @@
                 ring_copy(mod(z + step, 8), step, j, lsend, lrecv, zright).wait_recv()
                 if step < 4 and j in LEFT[step]:
                     ring_left(step + 1, j).start()
+            for work in gaps[j : j + 1]:
+                work()
 
     for j in range(4):
         for jj in (3, 4) if j == 3 else (j,):
@@ -255,10 +265,10 @@
 
     def prepare_images(slot):
         band = lax.rem(slot, 4)
-        first = (origin(slot) // 4) * 16
+        first = (origin(slot) // 4) * (ROWS // 2)
 
         def rows(n):
-            return pl.ds(pl.multiple_of((HALF + n) * 32 + first, 16), 16)
+            return pl.ds(pl.multiple_of((HALF + n) * 16 + first, 16), 16)
 
         @pl.loop(0, TILES)
         def _(t):
@@ -297,7 +307,7 @@
 
         def load(t):
             lanes = pl.ds(pl.multiple_of(t * 128, 128), 128)
-            blocks = [rbuf[band, xx, cc, :, lanes].astype(F32) for xx in range(4) for cc in range(2)]
+            blocks = [rbuf[cc, band, xx, :, lanes].astype(F32) for xx in range(4) for cc in range(2)]
             return [jnp.concatenate([b[4 * q : 4 * q + 4] for b in blocks], axis=0) for q in range(4)]
 
         @pl.loop(0, SPLIT - 1)
@@ -317,43 +327,59 @@
         else:
             sbuf[...] += term
 
+    def score_half(slot):
+        band = lax.rem(slot, 4)
+        rows = pl.ds(pl.multiple_of((origin(slot) // 4) * (ROWS // 2), 16), ROWS // 2)
+        sbuf[rows, :] += nt_dot(xbuf[band, rows, :], wbuf[band])
+
     prepare_images(z)
     ring_step(1)
-    prepare_images(mod(z - 1, 8))
-    prepare_images(mod(z + 1, 8))
-
-    @pl.loop(1, 16)
-    def _(k):
-        refs_arrival(k).wait_recv()
-        refs_forward(k).start()
-
-    ring_step(2)
+
+    def refs_groups(*groups):
+        for g in groups:
+            refs_group(g)
+
+    ring_step(
+        2,
+        lambda: prepare_images(mod(z - 1, 8)),
+        lambda: prepare_images(mod(z + 1, 8)),
+        lambda: refs_groups(0, 1),
+        lambda: refs_groups(2, 3),
+    )
+    spares = []
+
+    def refs_ready(*groups):
+        for g in groups:
+            refs_forwarded(g).wait_recv()
+            spares.append(prepare_refs(mod(y - g, 4)).astype(BF16))
+
     prepare_images(mod(z - 2, 8))
     prepare_images(mod(z + 2, 8))
-
-    @pl.loop(0, 16)
-    def _(k):
-        refs_forwarded(k).wait_recv()
-
-    half = jnp.where(lax.broadcasted_iota(jnp.int32, (8, 128), 1) < 3, -0.5, 0.0).astype(BF16)
-    norms = jnp.zeros((8, 32), F32)
-    for band in range(BANDS):
-        norms += nt_dot(half, prepare_refs(band).astype(BF16))
-    norms = jnp.concatenate([norms] * SIDE, axis=1)
+    ring_step(
+        3,
+        lambda: refs_ready(0),
+        lambda: refs_ready(1),
+        lambda: refs_ready(2),
+        lambda: refs_ready(3),
+    )
     score_band(mod(z + 2, 4), True)
-
-    ring_step(3)
     prepare_images(mod(z - 3, 8))
     prepare_images(mod(z + 3, 8))
     score_band(mod(z + 1, 4), False)
     score_band(mod(z + 3, 4), False)
+    score_half(z)
+    half = jnp.where(lax.broadcasted_iota(jnp.int32, (8, 128), 1) < 3, -0.5, 0.0).astype(BF16)
+    norms = jnp.zeros((8, 32), F32)
+    for spare in spares:
+        norms += nt_dot(half, spare)
+    norms = jnp.concatenate([norms] * SIDE, axis=1)
     row = lax.broadcasted_iota(jnp.int32, (MASKW, ROWS), 0)
     lane = lax.broadcasted_iota(jnp.int32, (MASKW, ROWS), 1)
     spread = jnp.where(row == (lane >> 5) * 64 + 8 * z + ((lane & 31) >> 2), 1.0, 0.0).astype(BF16)
 
     ring_step(4)
     prepare_images(mod(z + 4, 8))
-    score_band(lax.rem(z, 4), False)
+    score_half(mod(z + 4, 8))
 
     kept = []
     for e in range(2):
@@ -365,12 +391,17 @@
 
     lane8 = lax.broadcasted_iota(jnp.int32, (8, 128), 1)
     message = jnp.zeros((8, 128), F32)
+
+    def line_of(q, dx):
+        first = (q // 2) * (ROWS // 2) + dx * 16 + (q % 2) * 8
+        return slice(first, first + 8)
+
     for q in range(4):
         e, block = q // 2, q % 2
         tiles = []
         for dx in range(SIDE):
             line = kept[e][2 * dx + block : 2 * dx + block + 1]
-            tiles.append(sbuf[dx * 32 + q * 8 : dx * 32 + q * 8 + 8, :] + norms - PENALTY * (BANDS - line))
+            tiles.append(sbuf[line_of(q, dx), :] + norms - PENALTY * (BANDS - line))
         peak = tiles[0]
         for tile in tiles[1:]:
             peak = jnp.maximum(peak, tile)
@@ -378,7 +409,7 @@
         mass = jnp.zeros((8, ROWS), F32)
         for dx in range(SIDE):
             raised = jnp.exp(tiles[dx] - peak)
-            sbuf[dx * 32 + q * 8 : dx * 32 + q * 8 + 8, :] = raised
+            sbuf[line_of(q, dx), :] = raised
             mass += raised
         mass = jnp.sum(mass, axis=1, keepdims=True)
         message = jnp.where(lane8 == q, peak, jnp.where(lane8 == 4 + q, mass, message))
@@ -391,12 +422,9 @@
         slot = mod(z - d, 8)
         return remote(zbuf.at[slot], zbuf.at[slot], zsend.at[d], zrecv.at[d], dev(y, slot, x, core))
 
-    @pl.loop(1, 8)
-    def _(d):
+    for d in (4, 3, 5, 2, 6, 1, 7):
         z_copy(d).start()
-
-    @pl.loop(1, 8)
-    def _(d):
+    for d in (1, 7, 2, 6, 3, 5, 4):
         z_arrival(d).wait_recv()
 
     top = zbuf[0]
@@ -410,7 +438,7 @@
     for q in range(4):
         scale = factor[:, q : q + 1]
         for dx in range(SIDE):
-            sbuf[dx * 32 + q * 8 : dx * 32 + q * 8 + 8, :] = sbuf[dx * 32 + q * 8 : dx * 32 + q * 8 + 8, :] * scale
+            sbuf[line_of(q, dx), :] = sbuf[line_of(q, dx), :] * scale
     prob = sbuf[...].T
     post[...] = prob.astype(BF16)
     mass = jnp.sum(prob, axis=1, keepdims=True)
@@ -459,7 +487,7 @@
     def sums_band(k):
         band = mod(y + k, 4)
 
-        @pl.loop(0, SPLIT - 1)
+        @pl.loop(0, SPLIT - 1, unroll=6)
         def _(t):
             pack(band, t, sums_tile(band, t), sums_tile(band, t + SPLIT))
 
@@ -516,9 +544,8 @@
         refs_copy(k).wait_send()
         out_copy(k).wait_send()
 
-    @pl.loop(0, 16)
-    def _(k):
-        refs_forward(k).wait_send()
+    for g in range(4):
+        refs_forward(g).wait_send()
 
     @pl.loop(1, 8)
     def _(d):
@@ -546,7 +573,7 @@
             pltpu.VMEM((16, MASKW), F32),
             pltpu.VMEM((8, 16, BLOCK), BF16),
             pltpu.VMEM((16, PACK), F32),
-            pltpu.VMEM((BANDS, 4, 2, 16, PACK), BF16),
+            pltpu.VMEM((2, BANDS, 4, 16, PACK), BF16),
             pltpu.VMEM((BANDS, ROWS, 2 * COEF), BF16),
             pltpu.VMEM((BANDS, ROWS, 2 * COEF), BF16),
             pltpu.VMEM((ROWS, ROWS), F32),
@@ -557,7 +584,7 @@
             pltpu.VMEM((16, 16, PACK), BF16),
             dma((3,)), dma, dma((5,)), dma((5,)),
             dma((4, 4)), dma((4, 4)), dma((4, 4)), dma((4, 4)),
-            dma((16,)), dma((16,)), dma((16,)), dma((16,)),
+            dma((16,)), dma((16,)), dma((4,)), dma((4,)),
             dma((8,)), dma((8,)), dma((4,)), dma((4,)), dma((16,)), dma((16,)),
         ],
         compiler_params=pltpu.CompilerParams(

time: 61 us -> 57.9 us (0.949)
  Pallas kernels: 57.7 us -> 55.1 us
    pallas_call x1, Pallas kernels: 57.7 us -> 55.1 us  [per_device(): pl.pallas_call(kernel, out_shape=(jax.ShapeDtypeStruct((4, 2 * COEF), F32...]
where the time goes in v3:
time: 57.9 us; the launch traced here: 57.7 us
  Pallas kernels  55.1 us (95%)
  local copies, waits for them, and re-layouts  1.95 us (3%)
  between operations  0.65 us (1%)
    pallas_call x1, Pallas kernels, per_device(): pl.pallas_call(kernel, out_shape=(jax.ShapeDtypeStruct((4, 2 * COEF), F32...  55.1 us
    unnamed x4, local copies, waits for them, and re-layouts  1.95 us

profile of v3, /device:TPU:1, one launch (start us, length us, event | category | flops | bytes accessed | tf_op | source)
XLA Modules:
  0.0 57.7 jit_solution(8594515268336151032)
XLA Ops:
  0.6 55.1 %shard_map.68 = (f32[4,3328]{1,0:T(4,128)}, f32[1,4]{1,0:T(1,128)}) custom-call(bf16[16,3328]{1,0:T(8,128)(2,1)} %bitcast.7, bf16[4,3328]{1,0:T(4,128)(2,1)} %bitcast.10, f32[1,1664]{1,0:T(1,128)} %noise_hbm.1, s32[49,2,64]{2,1,0:T(2,128)} %bitcast.9, f32[8,8,1664]{2,1,0:T(8,128)} %constant.2.clone.tab_hbm), custom_call_target="tpu_custom_call" | custom-call | tf_op jit(solution)/shard_map/pallas_call | solution.py:562
  55.8 0.0 copy-start
  55.8 1.4 %copy.9 = f32[1,4,3328]{2,1,0:T(4,128)} copy(f32[1,4,3328]{2,1,0:T(4,128)} %bitcast.8) | data formatting | bytes 106496
  57.2 0.0 copy-done
  57.2 0.5 copy.10
Async XLA Ops:
  55.8 1.4 %copy-start = (f32[1,4]{1,0:T(1,128)S(1)}, f32[1,4]{1,0:T(1,128)}, u32[]{:S(2)}) copy-start(f32[1,4]{1,0:T(1,128)} %get-tuple-element.5) | copy-start | bytes 52

commit v4 on v3

--- a/solution.py
+++ b/solution.py
@@ -19,8 +19,8 @@
 SPLIT = 7
 PACK = SPLIT * 128
 MASKW = 512
-BLOCK = 2 * COEF + MASKW
-CHUNKS = ((0, 8), (8, 8), (16, 7), (23, 7))
+CHUNKS = ((0, 5), (5, 4), (9, 4), (13, 5), (18, 4), (22, 4))
+PIECES = len(CHUNKS)
 ROWS = 32 * SIDE
 F32 = jnp.float32
 BF16 = jnp.bfloat16
@@ -61,8 +61,8 @@
 def kernel(
     images_hbm, refs_hbm, noise_hbm, masks_hbm, tab_hbm,
     out_ref, tot_ref,
-    refs_ref, noise_ref, masks_ref, tab, stage, mcat, imgbuf, wpack, rbuf, xbuf, wbuf, sbuf, post, zbuf, obuf, cbuf, fbuf,
-    in_sem, tab_sem, tsend, trecv, rsend, rrecv, lsend, lrecv, wsend, wrecv, fsend, frecv,
+    refs_ref, noise_ref, masks_ref, tab, stage, mcat, mheld, mout, mpart, imgbuf, wpack, rbuf, xbuf, wbuf, sbuf, post, zbuf, obuf, cbuf, fbuf,
+    hsend, hrecv, msend, mrecv, in_sem, tab_sem, tsend, trecv, rsend, rrecv, lsend, lrecv, wsend, wrecv, fsend, frecv,
     zsend, zrecv, csend, crecv, osend, orecv,
 ):
     y = lax.axis_index("band")
@@ -74,12 +74,15 @@
     def dev(y, z, x, c):
         return (y, (z * 4 + x) * 2 + c)
 
+    def way(bands):
+        return mod(bands + 1 + core, 4) - 1 - core
+
     to_y = lax.rem(z, 4)
-    to_z = mod(z + mod(y - to_y + 1, 4) - 1, 8)
+    to_z = mod(z + way(y - to_y), 8)
     my_band = lax.rem(z, 4)
 
     def origin(slot):
-        return mod(slot - (mod(lax.rem(slot, 4) - y + 1, 4) - 1), 8)
+        return mod(slot - way(lax.rem(slot, 4) - y), 8)
 
     moved = to_y != y
     target = dev(to_y, to_z, x, core)
@@ -136,11 +139,7 @@
         return pl.ds(CHUNKS[j][0] * 128, CHUNKS[j][1] * 128)
 
     def piece(j, slot):
-        if j == 4:
-            return stage, imgbuf.at[slot, :, pl.ds(2 * COEF, MASKW)]
-        first = CHUNKS[j][0] * 128
-        lanes = pl.ds(first, min(CHUNKS[j][1] * 128, 2 * COEF - first))
-        return images_hbm.at[:, lanes], imgbuf.at[slot, :, lanes]
+        return images_hbm.at[:, lanes_of(j)], imgbuf.at[slot, :, lanes_of(j)]
 
     def move(j):
         return remote(*piece(j, to_z), tsend.at[j], trecv.at[j], target)
@@ -160,7 +159,7 @@
         def _():
             keep(j).start()
 
-    for j in range(4):
+    for j in range(PIECES):
         move_start(j)
 
     def refs_copy(k):
@@ -214,11 +213,17 @@
         dx, dy = s // SIDE, s % SIDE
         mcat[2 * dx : 2 * dx + 2, dy * 64 : dy * 64 + 64] = masks_ref[s].astype(F32)
     stage[...] = mcat[...].astype(BF16)
-
-    move_start(4)
-
-    RIGHT = [(0, 1, 2, 3)] * 3 + [(0, 1)]
-    LEFT = [(0, 1, 2, 3)] * 3 + [(2, 3)]
+    home_k = mod(to_y - y, 4)
+
+    def mask_copy(k, device):
+        return remote(stage, mheld.at[k - 1], hsend, hrecv.at[k - 1], device)
+
+    @pl.when(moved)
+    def _():
+        mask_copy(home_k, dev(to_y, z, x, core)).start()
+
+    RIGHT = [tuple(range(PIECES))] * 3 + [tuple(range(PIECES // 2))]
+    LEFT = [tuple(range(PIECES))] * 3 + [tuple(range(PIECES // 2, PIECES))]
 
     def ring_copy(slot, step, j, send, recv, device):
         ref = imgbuf.at[slot, :, lanes_of(j)]
@@ -231,7 +236,7 @@
         return ring_copy(mod(z + (step - 1), 8), step, j, lsend, lrecv, zleft)
 
     def ring_step(step, *gaps):
-        for j in range(4):
+        for j in range(PIECES):
             if j in RIGHT[step - 1]:
                 ring_copy(mod(z - step, 8), step, j, rsend, rrecv, zleft).wait_recv()
                 if step < 4 and j in RIGHT[step]:
@@ -243,19 +248,46 @@
             for work in gaps[j : j + 1]:
                 work()
 
-    for j in range(4):
-        for jj in (3, 4) if j == 3 else (j,):
-
-            @pl.when(moved)
-            def _():
-                moved_in(jj).wait_recv()
-
-            @pl.when(jnp.logical_not(moved))
-            def _():
-                keep(jj).wait()
+    for j in range(PIECES):
+
+        @pl.when(moved)
+        def _():
+            moved_in(j).wait_recv()
+
+        @pl.when(jnp.logical_not(moved))
+        def _():
+            keep(j).wait()
 
         ring_right(1, j).start()
         ring_left(1, j).start()
+
+    half_of = z // 4
+
+    def mask_part(d):
+        slot = mod(z + d, 8)
+        return remote(mout.at[slot], mpart.at[half_of], msend.at[d], mrecv.at[half_of], dev(y, slot, x, core))
+
+    def mask_arrival(e):
+        return remote(mpart.at[e], mpart.at[e], msend.at[0], mrecv.at[e], dev(y, mod(y + 4 * e, 8), x, core))
+
+    @pl.when(jnp.logical_not(moved))
+    def _():
+        total = mcat[...]
+        for k in range(1, 4):
+            mask_copy(k, dev(mod(y - k, 4), z, x, core)).wait_recv()
+            total += mheld[k - 1].astype(F32)
+        group = lax.broadcasted_iota(jnp.int32, (16, 128), 1) >> 3
+        for zd in range(8):
+            part = jnp.zeros((16, 128), F32)
+            for dy in range(SIDE):
+                tile = total[:, (dy // 2) * 128 : (dy // 2) * 128 + 128]
+                shift = (dy * 8 - (dy % 2) * 64 - 8 * zd) % 128
+                part = jnp.where(group == dy, pltpu.roll(tile, shift, 1) if shift else tile, part)
+            mout[zd] = part.astype(BF16)
+        mpart[half_of] = mout[z]
+        for d in (4, 3, 5, 2, 6, 1, 7):
+            mask_part(d).start()
+
     tab_copy.wait()
 
     def shifted(re, im, table, d):
@@ -373,21 +405,21 @@
     for spare in spares:
         norms += nt_dot(half, spare)
     norms = jnp.concatenate([norms] * SIDE, axis=1)
-    row = lax.broadcasted_iota(jnp.int32, (MASKW, ROWS), 0)
-    lane = lax.broadcasted_iota(jnp.int32, (MASKW, ROWS), 1)
-    spread = jnp.where(row == (lane >> 5) * 64 + 8 * z + ((lane & 31) >> 2), 1.0, 0.0).astype(BF16)
+    row = lax.broadcasted_iota(jnp.int32, (128, ROWS), 0)
+    lane = lax.broadcasted_iota(jnp.int32, (128, ROWS), 1)
+    spread = jnp.where(row == (lane >> 5) * 8 + ((lane & 31) >> 2), 1.0, 0.0).astype(BF16)
+    kept = []
+    for e in range(2):
+
+        @pl.when(z != mod(y + 4 * e, 8))
+        def _():
+            mask_arrival(e).wait_recv()
+
+        kept.append(jnp.dot(mpart[e], spread, preferred_element_type=F32))
 
     ring_step(4)
     prepare_images(mod(z + 4, 8))
     score_half(mod(z + 4, 8))
-
-    kept = []
-    for e in range(2):
-        total = jnp.zeros((16, MASKW), F32)
-        for band in range(BANDS):
-            slot = mod(y + 4 * e + mod(band - y + 1, 4) - 1, 8)
-            total += imgbuf[slot, :, 2 * COEF :].astype(F32)
-        kept.append(lax.dot_general(total.astype(BF16), spread, (((1,), (0,)), ((), ())), preferred_element_type=F32))
 
     lane8 = lax.broadcasted_iota(jnp.int32, (8, 128), 1)
     message = jnp.zeros((8, 128), F32)
@@ -530,8 +562,14 @@
 
     @pl.when(moved)
     def _():
-        for j in range(5):
+        for j in range(PIECES):
             move(j).wait_send()
+        mask_copy(home_k, dev(to_y, z, x, core)).wait_send()
+
+    @pl.when(jnp.logical_not(moved))
+    def _():
+        for d in range(1, 8):
+            mask_part(d).wait_send()
 
     for step in range(1, 5):
         for j in RIGHT[step - 1]:
@@ -571,7 +609,10 @@
             pltpu.VMEM((2 * BANDS, 8, COEF), F32),
             pltpu.VMEM((16, MASKW), BF16),
             pltpu.VMEM((16, MASKW), F32),
-            pltpu.VMEM((8, 16, BLOCK), BF16),
+            pltpu.VMEM((3, 16, MASKW), BF16),
+            pltpu.VMEM((8, 16, 128), BF16),
+            pltpu.VMEM((2, 16, 128), BF16),
+            pltpu.VMEM((8, 16, 2 * COEF), BF16),
             pltpu.VMEM((16, PACK), F32),
             pltpu.VMEM((2, BANDS, 4, 16, PACK), BF16),
             pltpu.VMEM((BANDS, ROWS, 2 * COEF), BF16),
@@ -582,8 +623,8 @@
             pltpu.VMEM((BANDS, 2, 4, 16, PACK), BF16),
             pltpu.VMEM((BANDS, 4, 16, PACK), BF16),
             pltpu.VMEM((16, 16, PACK), BF16),
-            dma((3,)), dma, dma((5,)), dma((5,)),
-            dma((4, 4)), dma((4, 4)), dma((4, 4)), dma((4, 4)),
+            dma, dma((3,)), dma((8,)), dma((2,)), dma((3,)), dma, dma((PIECES,)), dma((PIECES,)),
+            dma((4, PIECES)), dma((4, PIECES)), dma((4, PIECES)), dma((4, PIECES)),
             dma((16,)), dma((16,)), dma((4,)), dma((4,)),
             dma((8,)), dma((8,)), dma((4,)), dma((4,)), dma((16,)), dma((16,)),
         ],

time: 57.9 us -> 57.1 us (0.986)
  Pallas kernels: 55.1 us -> 54.3 us
    pallas_call x1, Pallas kernels: 55.1 us -> 54.3 us  [per_device(): pl.pallas_call(kernel, out_shape=(jax.ShapeDtypeStruct((4, 2 * COEF), F32...]
where the time goes in v4:
time: 57.1 us; the launch traced here: 56.9 us
  Pallas kernels  54.3 us (95%)
  local copies, waits for them, and re-layouts  1.95 us (3%)
  between operations  0.65 us (1%)
    pallas_call x1, Pallas kernels, per_device(): pl.pallas_call(kernel, out_shape=(jax.ShapeDtypeStruct((4, 2 * COEF), F32...  54.3 us
    unnamed x4, local copies, waits for them, and re-layouts  1.95 us

profile of v4, /device:TPU:1, one launch (start us, length us, event | category | flops | bytes accessed | tf_op | source)
XLA Modules:
  0.0 56.9 jit_solution(8549729951671511255)
XLA Ops:
  0.6 54.3 %shard_map.68 = (f32[4,3328]{1,0:T(4,128)}, f32[1,4]{1,0:T(1,128)}) custom-call(bf16[16,3328]{1,0:T(8,128)(2,1)} %bitcast.7, bf16[4,3328]{1,0:T(4,128)(2,1)} %bitcast.10, f32[1,1664]{1,0:T(1,128)} %noise_hbm.1, s32[49,2,64]{2,1,0:T(2,128)} %bitcast.9, f32[8,8,1664]{2,1,0:T(8,128)} %constant.2.clone.tab_hbm), custom_call_target="tpu_custom_call" | custom-call | tf_op jit(solution)/shard_map/pallas_call | solution.py:600
  55.0 0.0 copy-start
  55.0 1.4 %copy.9 = f32[1,4,3328]{2,1,0:T(4,128)} copy(f32[1,4,3328]{2,1,0:T(4,128)} %bitcast.8) | data formatting | bytes 106496
  56.4 0.0 copy-done
  56.4 0.5 copy.10
Async XLA Ops:
  55.0 1.4 %copy-start = (f32[1,4]{1,0:T(1,128)S(1)}, f32[1,4]{1,0:T(1,128)}, u32[]{:S(2)}) copy-start(f32[1,4]{1,0:T(1,128)} %get-tuple-element.5) | copy-start | bytes 52

commit v5 on v4

--- a/solution.py
+++ b/solution.py
@@ -359,11 +359,6 @@
         else:
             sbuf[...] += term
 
-    def score_half(slot):
-        band = lax.rem(slot, 4)
-        rows = pl.ds(pl.multiple_of((origin(slot) // 4) * (ROWS // 2), 16), ROWS // 2)
-        sbuf[rows, :] += nt_dot(xbuf[band, rows, :], wbuf[band])
-
     prepare_images(z)
     ring_step(1)
 
@@ -399,7 +394,6 @@
     prepare_images(mod(z + 3, 8))
     score_band(mod(z + 1, 4), False)
     score_band(mod(z + 3, 4), False)
-    score_half(z)
     half = jnp.where(lax.broadcasted_iota(jnp.int32, (8, 128), 1) < 3, -0.5, 0.0).astype(BF16)
     norms = jnp.zeros((8, 32), F32)
     for spare in spares:
@@ -419,7 +413,7 @@
 
     ring_step(4)
     prepare_images(mod(z + 4, 8))
-    score_half(mod(z + 4, 8))
+    score_band(lax.rem(z, 4), False)
 
     lane8 = lax.broadcasted_iota(jnp.int32, (8, 128), 1)
     message = jnp.zeros((8, 128), F32)

time: 57.1 us -> 56.1 us (0.982)
  Pallas kernels: 54.3 us -> 53.3 us
    pallas_call x1, Pallas kernels: 54.3 us -> 53.3 us  [per_device(): pl.pallas_call(kernel, out_shape=(jax.ShapeDtypeStruct((4, 2 * COEF), F32...]
where the time goes in v5:
time: 56.1 us; the launch traced here: 55.9 us
  Pallas kernels  53.3 us (95%)
  local copies, waits for them, and re-layouts  1.95 us (3%)
  between operations  0.65 us (1%)
    pallas_call x1, Pallas kernels, per_device(): pl.pallas_call(kernel, out_shape=(jax.ShapeDtypeStruct((4, 2 * COEF), F32...  53.3 us
    unnamed x4, local copies, waits for them, and re-layouts  1.95 us

profile of v5, /device:TPU:1, one launch (start us, length us, event | category | flops | bytes accessed | tf_op | source)
XLA Modules:
  0.0 55.9 jit_solution(13721192785066007341)
XLA Ops:
  0.6 53.3 %shard_map.68 = (f32[4,3328]{1,0:T(4,128)}, f32[1,4]{1,0:T(1,128)}) custom-call(bf16[16,3328]{1,0:T(8,128)(2,1)} %bitcast.7, bf16[4,3328]{1,0:T(4,128)(2,1)} %bitcast.10, f32[1,1664]{1,0:T(1,128)} %noise_hbm.1, s32[49,2,64]{2,1,0:T(2,128)} %bitcast.9, f32[8,8,1664]{2,1,0:T(8,128)} %constant.2.clone.tab_hbm), custom_call_target="tpu_custom_call" | custom-call | tf_op jit(solution)/shard_map/pallas_call | solution.py:594
  54.0 0.0 copy-start
  54.0 1.4 %copy.9 = f32[1,4,3328]{2,1,0:T(4,128)} copy(f32[1,4,3328]{2,1,0:T(4,128)} %bitcast.8) | data formatting | bytes 106496
  55.4 0.0 copy-done
  55.4 0.5 copy.10
Async XLA Ops:
  54.0 1.4 %copy-start = (f32[1,4]{1,0:T(1,128)S(1)}, f32[1,4]{1,0:T(1,128)}, u32[]{:S(2)}) copy-start(f32[1,4]{1,0:T(1,128)} %get-tuple-element.5) | copy-start | bytes 52
